TPU v7x, 32 devices: a whole 2x2x4 slice. The times are simulated.
32 devices in a mesh: grp: 2 (over y), row: 4 (over z), sub: 2 (over x), rhs: 2 (over core).
Axes of the slice: x: 2, y: 2, z: 4, core: 2. Of those that a mesh axis runs over, the one named last changes fastest.
Arguments:
- initial: float32 [128, 24576], P('rhs', ('grp', 'row', 'sub')), parts along dimension 1, as said below
- shifts: float32 [256], P(('grp', 'rhs')), parts along dimension 0, may hold values from 0.5 to 2
- send_list: int32 [16, 8], P('grp'), parts along dimension 0, may hold values from 0 to 5
- near_blocks: bfloat16 [768, 256, 256], P(('grp', 'row', 'sub')), parts along dimension 0, may hold values from -0.125 to 0.125
- near_row: int32 [768], P(('grp', 'row', 'sub')), parts along dimension 0, may hold values from 0 to 11, as said below
- near_src: int32 [768], P(('grp', 'row', 'sub')), parts along dimension 0, may hold values from 0 to 7
- far_u: bfloat16 [1536, 64, 256], P(('grp', 'row', 'sub')), parts along dimension 0, may hold values from -0.75 to 0.75
- far_v: bfloat16 [1536, 64, 256], P(('grp', 'row', 'sub')), parts along dimension 0, may hold values from -0.09375 to 0.09375
- far_row: int32 [1536], P(('grp', 'row', 'sub')), parts along dimension 0, may hold values from 0 to 11
- far_src: int32 [1536], P(('grp', 'row', 'sub')), parts along dimension 0, may hold values from 0 to 7, as said below
- far_rank: int32 [1536], P(('grp', 'row', 'sub')), parts along dimension 0, may hold values from 16 to 64
Outputs:
- second_basis: float32 [128, 24576], P('rhs', ('grp', 'row', 'sub')), parts along dimension 1
- residual: float32 [128, 24576], P('rhs', ('grp', 'row', 'sub')), parts along dimension 1
- hessenberg: float32 [4, 256], P(None, ('grp', 'rhs')), parts along dimension 1
There are 2 independent parts, one for each index of `grp`. A program takes and returns all parts, laid end to end along the dimension named above; each array names one. Nothing has to cross between parts.
Inputs may be any that keep to these rules, and one draw needn't show every extreme that they name: `send_list`: A local cluster index of the sending owner. `near_row`: on each device, its first 12 dense blocks name every row cluster of its group once; the others follow a uniform law. `near_src`: an owner index. `far_row`: row cluster inside the holder's group. `far_src`: on each device, its first 8 low-rank blocks name every owner once; the others follow a uniform law. `far_rank`: columns of the factors beyond the rank do not count. `initial`: real starting vectors.
All inputs are finite; a program needn't handle non-finite values.
Results may differ from a plain program's by a relative error of at most 0.0047.
Values may be sent and summed in bfloat16 or wider, within the bound.
A program may use at most 128 MiB of HBM per device.

v0:
```python
import jax
import jax.numpy as jnp
from jax import lax
from jax.sharding import PartitionSpec as P

epsilon = 1e-06


def local(
    initial,
    shifts,
    send_list,
    near_blocks,
    near_row,
    near_src,
    far_u,
    far_v,
    far_row,
    far_src,
    far_rank,
):
    row_count = lax.axis_size("row")
    sub_count = lax.axis_size("sub")
    owners = row_count * sub_count
    row_index = lax.axis_index("row")
    sub_index = lax.axis_index("sub")
    own_index = row_index * sub_count + sub_index
    local_rhs, width = initial.shape
    block = near_blocks.shape[1]
    rank_pad = far_u.shape[1]
    local_clusters = width // block
    group_clusters = local_clusters * sub_count
    total_panels = width * owners
    sources = jnp.arange(owners, dtype=jnp.int32)
    incoming = jnp.take(send_list, own_index, axis=1)
    group_ids = jnp.arange(group_clusters, dtype=jnp.int32)[:, None]
    near_pick = (near_row[None, :] == group_ids).astype(jnp.float32)
    far_pick = (far_row[None, :] == group_ids).astype(jnp.float32)
    live = jnp.arange(rank_pad, dtype=jnp.int32)[None, None, :] < far_rank[:, None, None]

    def fetch_columns(rounded):
        full = lax.all_gather(rounded, ("row", "sub"), axis=0, tiled=True)
        return full[sources * local_clusters + incoming]

    def operate(vector):
        rounded = (
            vector.astype(jnp.bfloat16).reshape(local_rhs, local_clusters, block).transpose(1, 0, 2)
        )
        columns = fetch_columns(rounded)
        near_y = jnp.einsum(
            "nlc,nrc->nlr", columns[near_src], near_blocks, preferred_element_type=jnp.float32
        )
        coefficients = jnp.einsum(
            "nlc,nkc->nlk", columns[far_src], far_v, preferred_element_type=jnp.float32
        )
        coefficients = jnp.where(live, coefficients, 0.0).astype(jnp.bfloat16)
        far_y = jnp.einsum("nlk,nkr->nlr", coefficients, far_u, preferred_element_type=jnp.float32)
        partial_sum = jnp.einsum("gn,nlr->glr", near_pick, near_y, precision=lax.Precision.HIGHEST)
        partial_sum = partial_sum + jnp.einsum(
            "gn,nlr->glr", far_pick, far_y, precision=lax.Precision.HIGHEST
        )
        owned = lax.psum_scatter(partial_sum, "sub", scatter_dimension=0, tiled=True)
        return owned.transpose(1, 0, 2).reshape(local_rhs, width) + shifts[:, None] * vector

    squares = lax.psum(jnp.sum(initial * initial, axis=1), ("row", "sub"))
    beta = jnp.sqrt(squares / total_panels + epsilon)
    first = initial / beta[:, None]
    image = operate(first)
    first_coef = lax.psum(jnp.sum(first * image, axis=1), ("row", "sub")) / total_panels
    remainder = image - first_coef[:, None] * first
    length_sum = lax.psum(jnp.sum(remainder * remainder, axis=1), ("row", "sub"))
    length_coef = jnp.sqrt(length_sum / total_panels + epsilon)
    second_basis = remainder / length_coef[:, None]
    image_next = operate(second_basis)
    sums_second = lax.psum(
        (jnp.sum(first * image_next, axis=1), jnp.sum(second_basis * image_next, axis=1)),
        ("row", "sub"),
    )
    cross_coef = sums_second[0] / total_panels
    second_coef = sums_second[1] / total_panels
    residual = image_next - cross_coef[:, None] * first - second_coef[:, None] * second_basis
    hessenberg = jnp.stack([first_coef, length_coef, cross_coef, second_coef])
    return (second_basis, residual, hessenberg)


def solution(mesh):
    placed = (
        P("rhs", ("grp", "row", "sub")),
        P(("grp", "rhs")),
        P("grp", None),
        P(("grp", "row", "sub"), None, None),
        P(("grp", "row", "sub")),
        P(("grp", "row", "sub")),
        P(("grp", "row", "sub"), None, None),
        P(("grp", "row", "sub"), None, None),
        P(("grp", "row", "sub")),
        P(("grp", "row", "sub")),
        P(("grp", "row", "sub")),
    )
    return jax.shard_map(
        local,
        mesh=mesh,
        in_specs=placed,
        out_specs=(
            P("rhs", ("grp", "row", "sub")),
            P("rhs", ("grp", "row", "sub")),
            P(None, ("grp", "rhs")),
        ),
        check_vma=False,
    )
```

profile of v0, /device:TPU:0, one launch (start us, length us, event | category | flops | bytes accessed | tf_op | source)
XLA Modules:
  0.0 301.2 jit_solution(3614993109419211708)
XLA Ops:
  8.5 23.1 %psum.35 = f32[64]{0:T(128)S(1)} all-reduce(f32[64]{0:T(128)S(1)} %multiply_reduce_fusion.4), channel_id=1, replica_groups=mesh['grp'=2,'row'=4,'sub'=2,'rhs'=2] {'row','sub'}, use_global_device_ids=true, to_apply=%region_1.2 | all-reduce | flops 64 | bytes 512 | tf_op jit(solution)/shard_map/psum | solution.py:65
  38.3 38.6 %all-gather.3.cloned.1.call-done = bf16[48,64,256]{2,1,0:T(8,128)(2,1)} async-done(((bf16[6,64,256]{2,1,0:T(8,128)(2,1)}), bf16[48,64,256]{2,1,0:T(8,128)(2,1)}) %all-gather.3.cloned.1.call-update) | async-done | bytes 1572880 | tf_op jit(solution)/shard_map/all_gather | solution.py:42
  76.9 2.0 gather_fusion
  78.9 2.6 gather_fusion.2
  81.5 1.9 gather_fusion.1
  83.4 7.3 %fusion.8 = f32[96,64,256]{2,1,0:T(8,128)} fusion(bf16[96,64,256]{2,1,0:T(8,128)(2,1)S(1)} %copy-done, bf16[96,64,256]{2,1,0:T(8,128)(2,1)} %gather_fusion.2, bf16[96,64,256]{2,1,0:T(8,128)(2,1)} %param.18, pred[96,64]{1,0:T(8,128)(4,1)S(1)} %iota_compare_fusion), kind=kOutput, calls=%fused_computation.16 | convolution fusion | flops 403439616 | bytes 15734784 | tf_op jit(solution)/shard_map/nlk,nkr->nlr/dot_general | solution.py:57
  90.7 8.4 %fusion.2 = f32[12,64,256]{2,0,1:T(8,128)S(1)} fusion(f32[96,64,256]{2,1,0:T(8,128)} %fusion.8, s32[96]{0:T(128)S(1)} %copy-done.14), kind=kOutput, calls=%fused_computation.8 | convolution fusion | flops 226493568 | bytes 7078272 | tf_op jit(solution)/shard_map/gn,nlr->glr/dot_general | solution.py:59
  99.1 4.8 %fusion.35 = f32[48,64,256]{2,1,0:T(8,128)S(1)} fusion(bf16[48,64,256]{2,1,0:T(8,128)(2,1)S(1)} %copy-done.5, bf16[48,256,256]{2,1,0:T(8,128)(2,1)} %param.14), kind=kOutput, calls=%fused_computation.62 | convolution fusion | flops 402653184 | bytes 11010048 | tf_op jit(solution)/shard_map/nlc,nrc->nlr/dot_general | solution.py:50
  103.9 3.0 fusion.10
  108.3 16.4 %reduce-scatter.3.cloned.1.call-done = f32[6,64,256]{2,1,0:T(8,128)} async-done(((f32[12,64,256]{2,1,0:T(8,128)}), f32[6,64,256]{2,1,0:T(8,128)}) %reduce-scatter.3.cloned.1.call-update) | async-done | bytes 393232 | tf_op jit(solution)/shard_map/reduce_scatter | solution.py:62
  127.9 21.1 %psum.36 = f32[64]{0:T(128)} all-reduce(f32[64]{0:T(128)} %multiply_reduce_fusion.3), channel_id=1, replica_groups=mesh['grp'=2,'row'=4,'sub'=2,'rhs'=2] {'row','sub'}, use_global_device_ids=true, to_apply=%region_4.5 | all-reduce | flops 64 | bytes 512 | tf_op jit(solution)/shard_map/psum | solution.py:69
  152.5 17.9 %psum.37 = f32[64]{0:T(128)} all-reduce(f32[64]{0:T(128)} %multiply_reduce_fusion.2), channel_id=1, replica_groups=mesh['grp'=2,'row'=4,'sub'=2,'rhs'=2] {'row','sub'}, use_global_device_ids=true, to_apply=%region_6.7 | all-reduce | flops 64 | bytes 512 | tf_op jit(solution)/shard_map/psum | solution.py:71
  171.6 2.0 fusion.34
  175.6 43.0 %all-gather.5.cloned.1.call-done = bf16[48,64,256]{2,1,0:T(8,128)(2,1)} async-done(((bf16[6,64,256]{2,1,0:T(8,128)(2,1)}), bf16[48,64,256]{2,1,0:T(8,128)(2,1)}) %all-gather.5.cloned.1.call-update) | async-done | bytes 1572880 | tf_op jit(solution)/shard_map/all_gather | solution.py:42
  218.5 2.1 gather_fusion.3
  220.6 2.7 gather_fusion.5
  223.3 2.0 gather_fusion.4
  225.4 7.3 %fusion.9 = f32[96,64,256]{2,1,0:T(8,128)} fusion(bf16[96,64,256]{2,1,0:T(8,128)(2,1)S(1)} %copy-done, bf16[96,64,256]{2,1,0:T(8,128)(2,1)} %gather_fusion.5, bf16[96,64,256]{2,1,0:T(8,128)(2,1)} %param.18, pred[96,64]{1,0:T(8,128)(4,1)S(1)} %iota_compare_fusion), kind=kOutput, calls=%fused_computation.17 | convolution fusion | flops 403439616 | bytes 15734784 | tf_op jit(solution)/shard_map/nlk,nkr->nlr/dot_general | solution.py:57
  232.7 8.4 %fusion = f32[12,64,256]{2,0,1:T(8,128)S(1)} fusion(f32[96,64,256]{2,1,0:T(8,128)} %fusion.9, s32[96]{0:T(128)S(1)} %copy-done.15), kind=kOutput, calls=%fused_computation.6 | convolution fusion | flops 226493568 | bytes 7078272 | tf_op jit(solution)/shard_map/gn,nlr->glr/dot_general | solution.py:59
  241.1 4.8 %fusion.36 = f32[48,64,256]{2,1,0:T(8,128)S(1)} fusion(bf16[48,64,256]{2,1,0:T(8,128)(2,1)S(1)} %copy-done.4, bf16[48,256,256]{2,1,0:T(8,128)(2,1)} %param.14), kind=kOutput, calls=%fused_computation.63 | convolution fusion | flops 402653184 | bytes 11010048 | tf_op jit(solution)/shard_map/nlc,nrc->nlr/dot_general | solution.py:50
  245.9 3.0 fusion.13
  250.3 16.4 %reduce-scatter.5.cloned.1.call-done = f32[6,64,256]{2,1,0:T(8,128)} async-done(((f32[12,64,256]{2,1,0:T(8,128)}), f32[6,64,256]{2,1,0:T(8,128)}) %reduce-scatter.5.cloned.1.call-update) | async-done | bytes 393232 | tf_op jit(solution)/shard_map/reduce_scatter | solution.py:62
  269.7 21.0 %all-reduce = (f32[64]{0:T(128)}, f32[64]{0:T(128)}) all-reduce(f32[64]{0:T(128)S(1)} %get-tuple-element.15, f32[64]{0:T(128)S(1)} %get-tuple-element.14), channel_id=1, replica_groups=mesh['grp'=2,'row'=4,'sub'=2,'rhs'=2] {'row','sub'}, use_global_device_ids=true, to_apply=%region_11.12 | all-reduce | flops 128 | bytes 1024 | tf_op jit(solution)/shard_map/psum | solution.py:75
  291.4 2.0 multiply_subtract_fusion
  (65 shorter events, 25.6 us)
Async XLA Ops:
  7.2 76.2 %copy-start = (bf16[96,64,256]{2,1,0:T(8,128)(2,1)S(1)}, bf16[96,64,256]{2,1,0:T(8,128)(2,1)}, u32[]{:S(2)}) copy-start(bf16[96,64,256]{2,1,0:T(8,128)(2,1)} %param.17) | copy-start | bytes 9437188
  7.2 69.7 %all-gather.3.cloned.1.call-start = ((), (), s32[]{:S(2)}) async-start(), calls=%async_computation.2 | async-start | bytes 1769472 | tf_op jit(solution)/shard_map/all_gather | solution.py:42
  35.3 89.4 %reduce-scatter.3.cloned.1.call-start = ((), (), s32[]{:S(2)}) async-start(), calls=%async_computation.3 | async-start | bytes 1179648 | tf_op jit(solution)/shard_map/reduce_scatter | solution.py:62
  36.2 45.2 %copy-start.8 = (s32[1024]{0:T(1024)}, s32[1024]{0:T(1024)S(1)}, u32[]{:S(2)}) copy-start(s32[1024]{0:T(1024)S(1)} %pad_clamp_fusion.2) | copy-start | bytes 12292
  36.9 44.6 %copy-start.9 = (s32[1024]{0:T(1024)}, s32[1024]{0:T(1024)S(1)}, u32[]{:S(2)}) copy-start(s32[1024]{0:T(1024)S(1)} %pad_clamp_fusion) | copy-start | bytes 12292
  37.6 43.9 %copy-start.10 = (s32[1024]{0:T(1024)}, s32[1024]{0:T(1024)S(1)}, u32[]{:S(2)}) copy-start(s32[1024]{0:T(1024)S(1)} %pad_clamp_fusion.1) | copy-start | bytes 12292
  83.4 7.3 %copy-start.14 = (s32[96]{0:T(128)S(1)}, s32[96]{0:T(128)}, u32[]{:S(2)}) copy-start(s32[96]{0:T(128)} %param.19) | copy-start | bytes 1156
  90.7 8.4 %copy-start.5 = (bf16[48,64,256]{2,1,0:T(8,128)(2,1)S(1)}, bf16[48,64,256]{2,1,0:T(8,128)(2,1)}, u32[]{:S(2)}) copy-start(bf16[48,64,256]{2,1,0:T(8,128)(2,1)} %gather_fusion.1) | copy-start | bytes 4718596
  99.1 4.8 %copy-start.12 = (s32[48]{0:T(128)S(1)}, s32[48]{0:T(128)}, u32[]{:S(2)}) copy-start(s32[48]{0:T(128)} %param.15) | copy-start | bytes 580
  103.9 22.5 %copy-start.1 = (f32[64,1536]{1,0:T(8,128)S(1)}, f32[64,1536]{1,0:T(8,128)}, u32[]{:S(2)}) copy-start(f32[64,1536]{1,0:T(8,128)} %param.11) | copy-start | bytes 1179652
  108.3 110.2 %all-gather.5.cloned.1.call-start = ((), (), s32[]{:S(2)}) async-start(), calls=%async_computation.4 | async-start | bytes 1769472 | tf_op jit(solution)/shard_map/all_gather | solution.py:42
  125.7 0.7 copy-start.3
  150.2 0.6 copy-start.11
  175.5 91.2 %reduce-scatter.5.cloned.1.call-start = ((), (), s32[]{:S(2)}) async-start(), calls=%async_computation.5 | async-start | bytes 1179648 | tf_op jit(solution)/shard_map/reduce_scatter | solution.py:62
  225.4 7.3 %copy-start.15 = (s32[96]{0:T(128)S(1)}, s32[96]{0:T(128)}, u32[]{:S(2)}) copy-start(s32[96]{0:T(128)} %param.19) | copy-start | bytes 1156
  232.7 8.4 %copy-start.4 = (bf16[48,64,256]{2,1,0:T(8,128)(2,1)S(1)}, bf16[48,64,256]{2,1,0:T(8,128)(2,1)}, u32[]{:S(2)}) copy-start(bf16[48,64,256]{2,1,0:T(8,128)(2,1)} %gather_fusion.4) | copy-start | bytes 4718596
  241.1 4.8 %copy-start.13 = (s32[48]{0:T(128)S(1)}, s32[48]{0:T(128)}, u32[]{:S(2)}) copy-start(s32[48]{0:T(128)} %param.15) | copy-start | bytes 580
  245.9 22.6 %copy-start.2 = (f32[64,1536]{1,0:T(8,128)S(1)}, f32[64,1536]{1,0:T(8,128)}, u32[]{:S(2)}) copy-start(f32[64,1536]{1,0:T(8,128)} %param.11) | copy-start | bytes 1179652
  245.9 22.5 %copy-start.7 = (f32[64]{0:T(128)S(1)}, f32[64]{0:T(128)}, u32[]{:S(2)}) copy-start(f32[64]{0:T(128)} %param.12) | copy-start | bytes 772
  267.7 0.7 copy-start.6
Sparse Core Ops, SparseCore 0:
  35.4 41.4 all-gather.2
  108.4 16.2 reduce-scatter.2
  175.6 42.8 all-gather.4
  250.4 16.2 reduce-scatter.4
where the time goes:
time: 302 us; the launch traced here: 301 us
  waiting for transfers between devices  114 us (38%)
  blocking collectives  83.1 us (28%)
  matrix products  47 us (16%)
  local copies, waits for them, and re-layouts  23.8 us (8%)
  other arithmetic  18.8 us (6%)
  between operations  14 us (5%)
    all_gather x2, waiting for transfers between devices, fetch_columns(): full = lax.all_gather(rounded, ('row', 'sub'), axis=0, tiled=True)  81.6 us
    reduce_scatter x2, waiting for transfers between devices, operate(): lax.psum_scatter(partial_sum, 'sub', scatter_dimension=0, tiled=True)  32.8 us
    psum x1, blocking collectives, local(): squares = lax.psum(jnp.sum(initial * initial, axis=1), ('row', 'sub'))  23.1 us
    psum x1, blocking collectives, local(): lax.psum(jnp.sum(first * image, axis=1), ('row', 'sub')) / total_panels  21.1 us
    psum x1, blocking collectives, local(): lax.psum((jnp.sum(first * image_next, axis=1), jnp.sum(second_basis * ima...  21 us
    psum x1, blocking collectives, local(): lax.psum(jnp.sum(remainder * remainder, axis=1), ('row', 'sub'))  17.9 us
    dot_general x2, matrix products, operate(): jnp.einsum('gn,nlr->glr', far_pick, far_y, precision=lax.Precision.HIGHEST)  16.8 us
    dot_general x2, matrix products, operate(): jnp.einsum('nlk,nkr->nlr', coefficients, far_u, preferred_element_type=jn...  14.6 us
  transfers between devices with their start and end apart: 4, of which 4 were waited for; matrix products, arithmetic and copies ran while one was open for 1% of the time, Pallas kernels for 0%

commit v1 on v0

v1 whole, which is shorter than its diff:
```python
import functools

import jax
import jax.numpy as jnp
from jax import lax
from jax.experimental import pallas as pl
from jax.experimental.pallas import tpu as pltpu
from jax.sharding import PartitionSpec as P

epsilon = 1e-06
CHUNKS = 2
UNROLL = 4
NT = (((1,), (1,)), ((), ()))
NN = (((1,), (0,)), ((), ()))


def arnoldi_kernel(
    row_count,
    sub_count,
    near_src,
    far_src,
    far_rank,
    chain,
    send_list,
    shifts_ref,
    x_ref,
    near_hbm,
    far_u_hbm,
    far_v_hbm,
    second_ref,
    resid_ref,
    hess_ref,
    near_v,
    u_v,
    v_v,
    rounded,
    staged,
    cols,
    coef,
    total,
    own_part,
    part_send,
    part_recv,
    image,
    dot_send,
    dot_recv,
    load_sem,
    col_send_sem,
    col_recv_sem,
    part_send_sem,
    part_recv_sem,
    dot_send_sem,
    dot_recv_sem,
):
    owners = row_count * sub_count
    row_index = lax.axis_index("row")
    sub_index = lax.axis_index("sub")
    me = row_index * sub_count + sub_index
    local_clusters, local_rhs, block = image.shape
    near_count = near_v.shape[0]
    far_count = u_v.shape[0]
    rank_pad = u_v.shape[1]
    blocks = near_count + far_count
    rows = local_rhs // CHUNKS
    panels = float(local_clusters * block * owners)

    def owner_id(offset):
        target = lax.rem(me + offset, owners)
        return {"row": target // sub_count, "sub": lax.rem(target, sub_count)}

    loads = [
        pltpu.make_async_copy(far_v_hbm, v_v, load_sem.at[0]),
        pltpu.make_async_copy(near_hbm, near_v, load_sem.at[1]),
        pltpu.make_async_copy(far_u_hbm, u_v, load_sem.at[2]),
    ]
    for load in loads:
        load.start()

    barrier = pltpu.get_barrier_semaphore()

    def greet(offset, carry):
        pl.semaphore_signal(
            barrier, inc=1, device_id=owner_id(offset), device_id_type=pl.DeviceIdType.MESH
        )
        return carry

    lax.fori_loop(1, owners, greet, 0)

    lanes = lax.broadcasted_iota(jnp.int32, (128, 128), 1)
    sublanes = lax.broadcasted_iota(jnp.int32, (128, 128), 0)
    diagonal = lanes == sublanes

    def to_column(line):
        return jnp.sum(jnp.where(diagonal, line, 0.0), axis=1, keepdims=True)

    def to_line(column):
        return jnp.sum(jnp.where(diagonal, column, 0.0), axis=0, keepdims=True)

    def part(chunk):
        return pl.ds(chunk * rows, rows)

    def send_columns(stage, chunk):
        def one(offset, carry):
            target = lax.rem(me + offset, owners)
            picked = send_list[me, target]
            staged[stage, chunk, offset] = rounded[stage, picked, part(chunk), :]
            pltpu.make_async_remote_copy(
                src_ref=staged.at[stage, chunk, offset],
                dst_ref=cols[stage][chunk].at[offset],
                send_sem=col_send_sem.at[stage, chunk],
                recv_sem=col_recv_sem.at[stage, chunk],
                device_id=owner_id(offset),
                device_id_type=pl.DeviceIdType.MESH,
            ).start()
            return carry

        lax.fori_loop(1, owners, one, 0)
        cols[stage][chunk][0] = rounded[stage, send_list[me, me], part(chunk), :]

    def send_dots(stage, chunk, values):
        pad = 128 - rows * len(values)
        column = jnp.concatenate(values + [jnp.zeros((pad, 1), jnp.float32)], axis=0)
        line = jnp.broadcast_to(to_line(column), (8, 128))
        dot_send[stage, chunk] = line
        dot_recv[stage, chunk, 0] = line

        def one(offset, carry):
            pltpu.make_async_remote_copy(
                src_ref=dot_send.at[stage, chunk],
                dst_ref=dot_recv.at[stage, chunk, offset],
                send_sem=dot_send_sem.at[stage, chunk],
                recv_sem=dot_recv_sem.at[stage, chunk],
                device_id=owner_id(offset),
                device_id_type=pl.DeviceIdType.MESH,
            ).start()
            return carry

        lax.fori_loop(1, owners, one, 0)

    def wait_bytes(ref, sem):
        pltpu.make_async_copy(ref, ref, sem).wait()

    def wait_dots(stage, chunk, count):
        wait_bytes(
            dot_recv.at[stage, chunk, pl.ds(1, owners - 1)], dot_recv_sem.at[stage, chunk]
        )

        def add(owner, acc):
            return acc + dot_recv[stage, chunk, lax.rem(me + owners - owner, owners)]

        line = lax.fori_loop(0, owners, add, jnp.zeros((8, 128), jnp.float32))
        column = to_column(line[0:1, :]) / panels
        return [column[k * rows : (k + 1) * rows] for k in range(count)]

    def slot_of(source):
        away = me - source
        return jnp.where(away < 0, away + owners, away)

    def apply_blocks(stage, chunk):
        held = cols[stage][chunk]
        wait_bytes(held.at[pl.ds(1, owners - 1)], col_recv_sem.at[stage, chunk])
        live = lax.broadcasted_iota(jnp.int32, (rows, rank_pad), 1)

        if stage == 0 and chunk == 0:
            loads[0].wait()

        def right_factors(step, carry):
            for j in range(UNROLL):
                n = step * UNROLL + j
                c = lax.dot_general(
                    held[slot_of(far_src[n])],
                    v_v[n],
                    NT,
                    preferred_element_type=jnp.float32,
                )
                coef[n] = jnp.where(live < far_rank[n], c, 0.0).astype(jnp.bfloat16)
            return carry

        lax.fori_loop(0, far_count // UNROLL, right_factors, 0)

        if stage == 0 and chunk == 0:
            loads[1].wait()

        def dense(step, carry):
            results = []
            for j in range(UNROLL):
                n = step * UNROLL + j
                results.append(
                    lax.dot_general(
                        held[slot_of(near_src[n])],
                        near_v[n],
                        NT,
                        preferred_element_type=jnp.float32,
                    )
                )
            for j in range(UNROLL):
                n = step * UNROLL + j
                total[n] = results[j] + total[chain[n]]
            return carry

        lax.fori_loop(0, near_count // UNROLL, dense, 0)

        if stage == 0 and chunk == 0:
            loads[2].wait()

        def left_factors(step, carry):
            results = []
            for j in range(UNROLL):
                n = step * UNROLL + j
                results.append(
                    lax.dot_general(coef[n], u_v[n], NN, preferred_element_type=jnp.float32)
                )
            for j in range(UNROLL):
                n = near_count + step * UNROLL + j
                total[n] = results[j] + total[chain[n]]
            return carry

        lax.fori_loop(0, far_count // UNROLL, left_factors, 0)

        for hop in range(1, sub_count):
            peer = lax.rem(sub_index + hop, sub_count)
            for q in range(local_clusters):
                last = chain[blocks + peer * local_clusters + q]
                part_send[stage, chunk, hop - 1, q] = total[last].astype(jnp.bfloat16)
            pltpu.make_async_remote_copy(
                src_ref=part_send.at[stage, chunk, hop - 1],
                dst_ref=part_recv.at[stage, chunk, hop - 1],
                send_sem=part_send_sem.at[stage, chunk],
                recv_sem=part_recv_sem.at[stage, chunk],
                device_id={"sub": peer},
                device_id_type=pl.DeviceIdType.MESH,
            ).start()
        for q in range(local_clusters):
            own_part[chunk, q] = total[chain[blocks + sub_index * local_clusters + q]]

    def gathered(stage, chunk, q):
        acc = own_part[chunk, q]
        for hop in range(sub_count - 1):
            acc = acc + part_recv[stage, chunk, hop, q].astype(jnp.float32)
        return acc

    def lane_sum(value):
        return jnp.sum(value, axis=1, keepdims=True)

    def span(q):
        return pl.ds(q * block, block)

    total[blocks] = jnp.zeros((rows, block), jnp.float32)
    for q in range(local_clusters):
        rounded[0, q] = x_ref[:, span(q)].astype(jnp.bfloat16)
    pl.semaphore_wait(barrier, owners - 1)
    for chunk in range(CHUNKS):
        send_columns(0, chunk)
        acc = jnp.zeros((rows, block), jnp.float32)
        for q in range(local_clusters):
            value = x_ref[part(chunk), span(q)]
            acc = acc + value * value
        send_dots(0, chunk, [lane_sum(acc)])

    for chunk in range(CHUNKS):
        apply_blocks(0, chunk)

    shift_line = jnp.concatenate(
        [shifts_ref[...], jnp.zeros((1, 128 - local_rhs), jnp.float32)], axis=1
    )
    shift_all = to_column(shift_line)
    shift = [shift_all[chunk * rows : (chunk + 1) * rows] for chunk in range(CHUNKS)]
    squares, inverse = [], []
    for chunk in range(CHUNKS):
        (mean_square,) = wait_dots(0, chunk, 1)
        inv_beta = 1.0 / jnp.sqrt(mean_square + epsilon)
        squares.append(mean_square)
        inverse.append(inv_beta)
        wait_bytes(part_recv.at[0, chunk], part_recv_sem.at[0, chunk])
        first_acc = jnp.zeros((rows, block), jnp.float32)
        self_acc = jnp.zeros((rows, block), jnp.float32)
        for q in range(local_clusters):
            value = gathered(0, chunk, q) * inv_beta
            image[q, part(chunk), :] = value
            rounded[1, q, part(chunk), :] = value.astype(jnp.bfloat16)
            first_acc = first_acc + (x_ref[part(chunk), span(q)] * inv_beta) * value
            self_acc = self_acc + value * value
        send_columns(1, chunk)
        send_dots(1, chunk, [lane_sum(first_acc), lane_sum(self_acc)])

    for chunk in range(CHUNKS):
        apply_blocks(1, chunk)

    coefficients = []
    for chunk in range(CHUNKS):
        inv_beta = inverse[chunk]
        first_image, image_square = wait_dots(1, chunk, 2)
        norm = squares[chunk] + epsilon
        first_square = squares[chunk] / norm
        drift = first_image - shift[chunk] * (epsilon / norm)
        first_coef = shift[chunk] + drift
        length = image_square - 2.0 * drift * first_image + drift * drift * first_square
        length_coef = jnp.sqrt(jnp.maximum(length, 0.0) + epsilon)
        inv_length = 1.0 / length_coef
        coefficients.append((first_coef, length_coef))
        wait_bytes(part_recv.at[1, chunk], part_recv_sem.at[1, chunk])
        first_acc = jnp.zeros((rows, block), jnp.float32)
        second_acc = jnp.zeros((rows, block), jnp.float32)
        for q in range(local_clusters):
            base = image[q, part(chunk), :]
            first = x_ref[part(chunk), span(q)] * inv_beta
            second = (base - drift * first) * inv_length
            image_next = shift[chunk] * second + (gathered(1, chunk, q) - drift * base) * inv_length
            second_ref[part(chunk), span(q)] = second
            resid_ref[part(chunk), span(q)] = image_next
            first_acc = first_acc + first * image_next
            second_acc = second_acc + second * image_next
        send_dots(2, chunk, [lane_sum(first_acc), lane_sum(second_acc)])

    table = [[], [], [], []]
    for chunk in range(CHUNKS):
        cross_coef, second_coef = wait_dots(2, chunk, 2)
        cross_first = cross_coef * inverse[chunk]
        for q in range(local_clusters):
            resid_ref[part(chunk), span(q)] = (
                resid_ref[part(chunk), span(q)]
                - cross_first * x_ref[part(chunk), span(q)]
                - second_coef * second_ref[part(chunk), span(q)]
            )
        for entry, value in zip(table, coefficients[chunk] + (cross_coef, second_coef)):
            entry.append(value)
    for k in range(4):
        column = jnp.concatenate(
            table[k] + [jnp.zeros((128 - local_rhs, 1), jnp.float32)], axis=0
        )
        hess_ref[k : k + 1, :] = to_line(column)[:, :local_rhs]

    for chunk in range(CHUNKS):
        for stage in range(2):
            wait_bytes(
                staged.at[stage, chunk, pl.ds(1, owners - 1)], col_send_sem.at[stage, chunk]
            )
            wait_bytes(part_send.at[stage, chunk], part_send_sem.at[stage, chunk])
        for stage in range(3):
            wait_bytes(
                dot_recv.at[stage, chunk, pl.ds(1, owners - 1)], dot_send_sem.at[stage, chunk]
            )


def local(
    row_count,
    sub_count,
    initial,
    shifts,
    send_list,
    near_blocks,
    near_row,
    near_src,
    far_u,
    far_v,
    far_row,
    far_src,
    far_rank,
):
    owners = row_count * sub_count
    local_rhs, width = initial.shape
    near_count, block = near_blocks.shape[:2]
    far_count, rank_pad = far_u.shape[:2]
    clusters = width // block
    blocks = near_count + far_count
    rows = local_rhs // CHUNKS

    targets = jnp.concatenate([near_row, far_row])
    wanted = jnp.concatenate([targets, jnp.arange(clusters * sub_count, dtype=jnp.int32)])
    order = jnp.arange(blocks, dtype=jnp.int32)
    place = jnp.arange(wanted.shape[0], dtype=jnp.int32)
    same = (targets[None, :] == wanted[:, None]) & (order[None, :] < place[:, None])
    chain = jnp.max(jnp.where(same, order[None, :], -1), axis=1)
    chain = jnp.where(chain < 0, blocks, chain)

    smem = pl.BlockSpec(memory_space=pltpu.SMEM)
    vmem = pl.BlockSpec(memory_space=pltpu.VMEM)
    hbm = pl.BlockSpec(memory_space=pl.ANY)
    bf16, f32 = jnp.bfloat16, jnp.float32
    return pl.pallas_call(
        functools.partial(arnoldi_kernel, row_count, sub_count),
        out_shape=(
            jax.ShapeDtypeStruct((local_rhs, width), f32),
            jax.ShapeDtypeStruct((local_rhs, width), f32),
            jax.ShapeDtypeStruct((4, local_rhs), f32),
        ),
        in_specs=[smem] * 5 + [vmem] * 2 + [hbm] * 3,
        out_specs=(vmem, vmem, vmem),
        scratch_shapes=[
            pltpu.VMEM(near_blocks.shape, bf16),
            pltpu.VMEM(far_u.shape, bf16),
            pltpu.VMEM(far_v.shape, bf16),
            pltpu.VMEM((2, clusters, local_rhs, block), bf16),
            pltpu.VMEM((2, CHUNKS, owners, rows, block), bf16),
            [[pltpu.VMEM((owners, rows, block), bf16)] * CHUNKS] * 2,
            pltpu.VMEM((far_count, rows, rank_pad), bf16),
            pltpu.VMEM((blocks + 1, rows, block), f32),
            pltpu.VMEM((CHUNKS, clusters, rows, block), f32),
            pltpu.VMEM((2, CHUNKS, sub_count - 1, clusters, rows, block), bf16),
            pltpu.VMEM((2, CHUNKS, sub_count - 1, clusters, rows, block), bf16),
            pltpu.VMEM((clusters, local_rhs, block), f32),
            pltpu.VMEM((3, CHUNKS, 8, 128), f32),
            pltpu.VMEM((3, CHUNKS, owners, 8, 128), f32),
            pltpu.SemaphoreType.DMA((3,)),
            pltpu.SemaphoreType.DMA((2, CHUNKS)),
            pltpu.SemaphoreType.DMA((2, CHUNKS)),
            pltpu.SemaphoreType.DMA((2, CHUNKS)),
            pltpu.SemaphoreType.DMA((2, CHUNKS)),
            pltpu.SemaphoreType.DMA((3, CHUNKS)),
            pltpu.SemaphoreType.DMA((3, CHUNKS)),
        ],
        compiler_params=pltpu.CompilerParams(
            collective_id=0, has_side_effects=True, vmem_limit_bytes=56 * 1024 * 1024
        ),
    )(
        near_src,
        far_src,
        far_rank,
        chain,
        send_list,
        shifts.reshape(1, local_rhs),
        initial,
        near_blocks,
        far_u,
        far_v,
    )


def solution(mesh):
    placed = (
        P("rhs", ("grp", "row", "sub")),
        P(("grp", "rhs")),
        P("grp", None),
        P(("grp", "row", "sub"), None, None),
        P(("grp", "row", "sub")),
        P(("grp", "row", "sub")),
        P(("grp", "row", "sub"), None, None),
        P(("grp", "row", "sub"), None, None),
        P(("grp", "row", "sub")),
        P(("grp", "row", "sub")),
        P(("grp", "row", "sub")),
    )
    return jax.shard_map(
        functools.partial(local, mesh.shape["row"], mesh.shape["sub"]),
        mesh=mesh,
        in_specs=placed,
        out_specs=(
            P("rhs", ("grp", "row", "sub")),
            P("rhs", ("grp", "row", "sub")),
            P(None, ("grp", "rhs")),
        ),
        check_vma=False,
    )
```

time: 302 us -> 79.8 us (0.26)
  waiting for transfers between devices: 114 us -> 0 us
  blocking collectives: 83.1 us -> 0 us
  Pallas kernels: 0 us -> 71.9 us
  matrix products: 47 us -> 0 us
  local copies, waits for them, and re-layouts: 23.8 us -> 4.79 us
  other arithmetic: 18.8 us -> 2.18 us
  between operations: 14 us -> 0.65 us
    psum x4 -> x0, blocking collectives: 83.1 us -> none  [the longest x1 23.1 us: local(): squares = lax.psum(jnp.sum(initial * initial, axis=1), ('row', 'sub'))]
    all_gather x2 -> x0, waiting for transfers between devices: 81.6 us -> none  [fetch_columns(): full = lax.all_gather(rounded, ('row', 'sub'), axis=0, tiled=True)]
    pallas_call x0 -> x1, Pallas kernels: none -> 71.9 us  [local(): pl.pallas_call(functools.partial(arnoldi_kernel, row_count, sub_count), o...]
    dot_general x8 -> x0, matrix products: 47 us -> none  [the longest x2 16.8 us: operate(): jnp.einsum('gn,nlr->glr', far_pick, far_y, precision=lax.Precision.HIGHEST)]
    reduce_scatter x2 -> x0, waiting for transfers between devices: 32.8 us -> none  [operate(): lax.psum_scatter(partial_sum, 'sub', scatter_dimension=0, tiled=True)]
    gather x6 -> x0, local copies, waits for them, and re-layouts: 13.3 us -> none  [the longest x2 5.31 us: operate(): columns[far_src]]
    reduce_sum x4 -> x0, other arithmetic: 5.75 us -> none  [the longest x1 1.79 us: local(): jnp.sum(remainder * remainder, axis=1)]
    reshape x4 -> x0, local copies, waits for them, and re-layouts: 4.35 us -> none  [the longest x2 2.3 us: operate(): vector.astype(jnp.bfloat16).reshape(local_rhs, local_clusters, block)]
  transfers between devices with their start and end apart: 4 -> 0, of which waited for: 4 -> 0; matrix products, arithmetic and copies ran while one was open for 1% -> 0% of each run, Pallas kernels for 0% -> 0%
where the time goes in v1:
time: 79.8 us; the launch traced here: 79.6 us
  Pallas kernels  71.9 us (90%)
  local copies, waits for them, and re-layouts  4.79 us (6%)
  other arithmetic  2.18 us (3%)
    pallas_call x1, Pallas kernels, local(): pl.pallas_call(functools.partial(arnoldi_kernel, row_count, sub_count), o...  71.9 us
    unnamed x3, local copies, waits for them, and re-layouts  4.79 us

profile of v1, /device:TPU:0, one launch (start us, length us, event | category | flops | bytes accessed | tf_op | source)
XLA Modules:
  0.0 79.6 jit_solution(17539104675663811634)
XLA Ops:
  0.6 0.8 pad_add_fusion.1
  1.4 0.7 pad_add_fusion
  2.1 0.1 select_reduce_fusion
  2.2 0.6 compare_select_fusion.chain
  2.8 71.9 %shard_map.130 = (f32[64,1536]{1,0:T(8,128)}, f32[64,1536]{1,0:T(8,128)}, f32[4,64]{1,0:T(4,128)}) custom-call(s32[48]{0:T(128)} %near_src.1, s32[96]{0:T(128)} %far_src.1, s32[96]{0:T(128)} %far_rank.1, s32[156]{0:T(256)} %compare_select_fusion.chain, s32[8,8]{1,0:T(8,128)} %send_list.1, f32[1,64]{1,0:T(1,128)} %bitcast.1, f32[64,1536]{1,0:T(8,128)} %x_ref.1, ...), custom_call_target="tpu_custom_call" | custom-call | tf_op jit(solution)/shard_map/pallas_call | solution.py:380
  74.8 1.8 %copy.17 = f32[64,1536]{1,0:T(8,128)} copy(f32[64,1536]{1,0:T(8,128)} %get-tuple-element.6) | data formatting | bytes 786432
  76.5 1.8 %copy.18 = f32[64,1536]{1,0:T(8,128)} copy(f32[64,1536]{1,0:T(8,128)} %get-tuple-element.7) | data formatting | bytes 786432
  78.3 1.3 %copy.19 = f32[4,64]{1,0:T(4,128)} copy(f32[4,64]{1,0:T(4,128)} %get-tuple-element.8) | data formatting | bytes 2048
  (1 shorter events, 0.0 us)

commit v2 on v1

--- a/solution.py
+++ b/solution.py
@@ -9,7 +9,7 @@
 
 epsilon = 1e-06
 CHUNKS = 2
-UNROLL = 4
+UNROLL = 24
 NT = (((1,), (1,)), ((), ()))
 NN = (((1,), (0,)), ((), ()))
 

time: 79.8 us -> 54.4 us (0.68)
  Pallas kernels: 71.9 us -> 46.6 us
    pallas_call x1, Pallas kernels: 71.9 us -> 46.6 us  [local(): pl.pallas_call(functools.partial(arnoldi_kernel, row_count, sub_count), o...]
where the time goes in v2:
time: 54.4 us; the launch traced here: 54.2 us
  Pallas kernels  46.6 us (86%)
  local copies, waits for them, and re-layouts  4.79 us (9%)
  other arithmetic  2.18 us (4%)
  between operations  0.65 us (1%)
    pallas_call x1, Pallas kernels, local(): pl.pallas_call(functools.partial(arnoldi_kernel, row_count, sub_count), o...  46.6 us
    unnamed x3, local copies, waits for them, and re-layouts  4.79 us

profile of v2, /device:TPU:0, one launch (start us, length us, event | category | flops | bytes accessed | tf_op | source)
XLA Modules:
  0.0 54.2 jit_solution(10355569776259094353)
XLA Ops:
  0.6 0.8 %pad_add_fusion.1 = s32[156]{0:T(256)S(1)} fusion(s32[12]{0:T(128)S(1)} %iota.11, s32[96]{0:T(128)} %param.19, s32[48]{0:T(128)} %param.15), kind=kLoop, calls=%fused_computation.5 | loop fusion | flops 312 | bytes 1248 | tf_op jit(solution)/shard_map/concatenate | solution.py:369
  1.4 0.7 %pad_add_fusion = s32[144]{0:T(256)S(1)} fusion(s32[96]{0:T(128)} %param.19, s32[48]{0:T(128)} %param.15), kind=kLoop, calls=%fused_computation.4 | loop fusion | flops 144 | bytes 1152 | tf_op jit(solution)/shard_map/concatenate | solution.py:368
  2.1 0.1 select_reduce_fusion
  2.2 0.6 %compare_select_fusion.chain = s32[156]{0:T(256)} fusion(s32[156]{0:T(256)S(1)} %select_reduce_fusion), kind=kLoop, calls=%fused_computation.3 | loop fusion | flops 312 | bytes 1248 | tf_op jit(solution)/shard_map/jit(_where)/select_n | solution.py:374
  2.8 46.6 %shard_map.130 = (f32[64,1536]{1,0:T(8,128)}, f32[64,1536]{1,0:T(8,128)}, f32[4,64]{1,0:T(4,128)}) custom-call(s32[48]{0:T(128)} %near_src.1, s32[96]{0:T(128)} %far_src.1, s32[96]{0:T(128)} %far_rank.1, s32[156]{0:T(256)} %compare_select_fusion.chain, s32[8,8]{1,0:T(8,128)} %send_list.1, f32[1,64]{1,0:T(1,128)} %bitcast.1, f32[64,1536]{1,0:T(8,128)} %x_ref.1, ...), custom_call_target="tpu_custom_call" | custom-call | tf_op jit(solution)/shard_map/pallas_call | solution.py:380
  49.4 1.8 %copy.17 = f32[64,1536]{1,0:T(8,128)} copy(f32[64,1536]{1,0:T(8,128)} %get-tuple-element.6) | data formatting | bytes 786432
  51.2 1.8 %copy.18 = f32[64,1536]{1,0:T(8,128)} copy(f32[64,1536]{1,0:T(8,128)} %get-tuple-element.7) | data formatting | bytes 786432
  52.9 1.3 %copy.19 = f32[4,64]{1,0:T(4,128)} copy(f32[4,64]{1,0:T(4,128)} %get-tuple-element.8) | data formatting | bytes 2048
  (1 shorter events, 0.0 us)

commit v3 on v2

--- a/solution.py
+++ b/solution.py
@@ -28,8 +28,8 @@
     far_u_hbm,
     far_v_hbm,
     second_ref,
-    resid_ref,
-    hess_ref,
+    image_ref,
+    table_ref,
     near_v,
     u_v,
     v_v,
@@ -119,7 +119,7 @@
 
     def send_dots(stage, chunk, values):
         pad = 128 - rows * len(values)
-        column = jnp.concatenate(values + [jnp.zeros((pad, 1), jnp.float32)], axis=0)
+        column = jnp.concatenate(values + ([jnp.zeros((pad, 1), jnp.float32)] if pad else []), axis=0)
         line = jnp.broadcast_to(to_line(column), (8, 128))
         dot_send[stage, chunk] = line
         dot_recv[stage, chunk, 0] = line
@@ -156,9 +156,11 @@
         away = me - source
         return jnp.where(away < 0, away + owners, away)
 
-    def apply_blocks(stage, chunk):
+    def wait_columns(stage, chunk):
+        wait_bytes(cols[stage][chunk].at[pl.ds(1, owners - 1)], col_recv_sem.at[stage, chunk])
+
+    def apply_right_and_dense(stage, chunk):
         held = cols[stage][chunk]
-        wait_bytes(held.at[pl.ds(1, owners - 1)], col_recv_sem.at[stage, chunk])
         live = lax.broadcasted_iota(jnp.int32, (rows, rank_pad), 1)
 
         if stage == 0 and chunk == 0:
@@ -200,6 +202,7 @@
 
         lax.fori_loop(0, near_count // UNROLL, dense, 0)
 
+    def apply_left(stage, chunk):
         if stage == 0 and chunk == 0:
             loads[2].wait()
 
@@ -248,8 +251,15 @@
     total[blocks] = jnp.zeros((rows, block), jnp.float32)
     for q in range(local_clusters):
         rounded[0, q] = x_ref[:, span(q)].astype(jnp.bfloat16)
+    shift_line = jnp.concatenate(
+        [shifts_ref[...], jnp.zeros((1, 128 - local_rhs), jnp.float32)], axis=1
+    )
+    shift_all = to_column(shift_line)
+    shift = [shift_all[chunk * rows : (chunk + 1) * rows] for chunk in range(CHUNKS)]
+    squares, inverse, coefficients = [], [], []
     pl.semaphore_wait(barrier, owners - 1)
-    for chunk in range(CHUNKS):
+
+    def start(chunk):
         send_columns(0, chunk)
         acc = jnp.zeros((rows, block), jnp.float32)
         for q in range(local_clusters):
@@ -257,16 +267,7 @@
             acc = acc + value * value
         send_dots(0, chunk, [lane_sum(acc)])
 
-    for chunk in range(CHUNKS):
-        apply_blocks(0, chunk)
-
-    shift_line = jnp.concatenate(
-        [shifts_ref[...], jnp.zeros((1, 128 - local_rhs), jnp.float32)], axis=1
-    )
-    shift_all = to_column(shift_line)
-    shift = [shift_all[chunk * rows : (chunk + 1) * rows] for chunk in range(CHUNKS)]
-    squares, inverse = [], []
-    for chunk in range(CHUNKS):
+    def first_image_of(chunk):
         (mean_square,) = wait_dots(0, chunk, 1)
         inv_beta = 1.0 / jnp.sqrt(mean_square + epsilon)
         squares.append(mean_square)
@@ -278,16 +279,14 @@
             value = gathered(0, chunk, q) * inv_beta
             image[q, part(chunk), :] = value
             rounded[1, q, part(chunk), :] = value.astype(jnp.bfloat16)
+        send_columns(1, chunk)
+        for q in range(local_clusters):
+            value = image[q, part(chunk), :]
             first_acc = first_acc + (x_ref[part(chunk), span(q)] * inv_beta) * value
             self_acc = self_acc + value * value
-        send_columns(1, chunk)
         send_dots(1, chunk, [lane_sum(first_acc), lane_sum(self_acc)])
 
-    for chunk in range(CHUNKS):
-        apply_blocks(1, chunk)
-
-    coefficients = []
-    for chunk in range(CHUNKS):
+    def second_image_of(chunk):
         inv_beta = inverse[chunk]
         first_image, image_square = wait_dots(1, chunk, 2)
         norm = squares[chunk] + epsilon
@@ -307,28 +306,35 @@
             second = (base - drift * first) * inv_length
             image_next = shift[chunk] * second + (gathered(1, chunk, q) - drift * base) * inv_length
             second_ref[part(chunk), span(q)] = second
-            resid_ref[part(chunk), span(q)] = image_next
+            image_ref[part(chunk), span(q)] = image_next
             first_acc = first_acc + first * image_next
             second_acc = second_acc + second * image_next
         send_dots(2, chunk, [lane_sum(first_acc), lane_sum(second_acc)])
 
-    table = [[], [], [], []]
+    start(0)
+    for stage, finish in ((0, first_image_of), (1, second_image_of)):
+        for chunk in range(CHUNKS):
+            wait_columns(stage, chunk)
+            if stage == 0 and chunk + 1 < CHUNKS:
+                start(chunk + 1)
+            apply_right_and_dense(stage, chunk)
+            if chunk > 0:
+                finish(chunk - 1)
+            apply_left(stage, chunk)
+        finish(CHUNKS - 1)
+
+    table = [[], [], [], [], []]
     for chunk in range(CHUNKS):
         cross_coef, second_coef = wait_dots(2, chunk, 2)
-        cross_first = cross_coef * inverse[chunk]
-        for q in range(local_clusters):
-            resid_ref[part(chunk), span(q)] = (
-                resid_ref[part(chunk), span(q)]
-                - cross_first * x_ref[part(chunk), span(q)]
-                - second_coef * second_ref[part(chunk), span(q)]
-            )
-        for entry, value in zip(table, coefficients[chunk] + (cross_coef, second_coef)):
+        values = coefficients[chunk] + (cross_coef, second_coef, cross_coef * inverse[chunk])
+        for entry, value in zip(table, values):
             entry.append(value)
-    for k in range(4):
+    for k in range(5):
         column = jnp.concatenate(
             table[k] + [jnp.zeros((128 - local_rhs, 1), jnp.float32)], axis=0
         )
-        hess_ref[k : k + 1, :] = to_line(column)[:, :local_rhs]
+        table_ref[k : k + 1, :] = to_line(column)
+    table_ref[5:8, :] = jnp.zeros((3, 128), jnp.float32)
 
     for chunk in range(CHUNKS):
         for stage in range(2):
@@ -340,6 +346,24 @@
             wait_bytes(
                 dot_recv.at[stage, chunk, pl.ds(1, owners - 1)], dot_send_sem.at[stage, chunk]
             )
+
+
+def finish_kernel(second_in, image_in, table_in, x_ref, second_ref, resid_ref, hess_ref):
+    rhs = x_ref.shape[0]
+    shape = (128, 128)
+    diagonal = lax.broadcasted_iota(jnp.int32, shape, 1) == lax.broadcasted_iota(
+        jnp.int32, shape, 0
+    )
+
+    def to_column(line):
+        return jnp.sum(jnp.where(diagonal, line, 0.0), axis=1, keepdims=True)[:rhs]
+
+    second_coef = to_column(table_in[3:4, :])
+    cross_first = to_column(table_in[4:5, :])
+    second = second_in[...]
+    second_ref[...] = second
+    resid_ref[...] = image_in[...] - cross_first * x_ref[...] - second_coef * second
+    hess_ref[...] = table_in[0:4, :rhs]
 
 
 def local(
@@ -377,12 +401,12 @@
     vmem = pl.BlockSpec(memory_space=pltpu.VMEM)
     hbm = pl.BlockSpec(memory_space=pl.ANY)
     bf16, f32 = jnp.bfloat16, jnp.float32
-    return pl.pallas_call(
+    second, image_next, table = pl.pallas_call(
         functools.partial(arnoldi_kernel, row_count, sub_count),
         out_shape=(
             jax.ShapeDtypeStruct((local_rhs, width), f32),
             jax.ShapeDtypeStruct((local_rhs, width), f32),
-            jax.ShapeDtypeStruct((4, local_rhs), f32),
+            jax.ShapeDtypeStruct((8, 128), f32),
         ),
         in_specs=[smem] * 5 + [vmem] * 2 + [hbm] * 3,
         out_specs=(vmem, vmem, vmem),
@@ -424,6 +448,16 @@
         far_u,
         far_v,
     )
+    return pl.pallas_call(
+        finish_kernel,
+        out_shape=(
+            jax.ShapeDtypeStruct((local_rhs, width), f32),
+            jax.ShapeDtypeStruct((local_rhs, width), f32),
+            jax.ShapeDtypeStruct((4, local_rhs), f32),
+        ),
+        in_specs=[vmem] * 4,
+        out_specs=(vmem, vmem, vmem),
+    )(second, image_next, table, initial)
 
 
 def solution(mesh):

time: 54.4 us -> 51.7 us (0.950)
  local copies, waits for them, and re-layouts: 4.79 us -> 0.01 us
  Pallas kernels: 46.6 us -> 48.7 us
    unnamed x3 -> x0, local copies, waits for them, and re-layouts: 4.79 us -> none
    pallas_call x0 -> x1, Pallas kernels: none -> 2.17 us  [local(): pl.pallas_call(finish_kernel, out_shape=(jax.ShapeDtypeStruct((local_rhs,...]
where the time goes in v3:
time: 51.7 us; the launch traced here: 51.5 us
  Pallas kernels  48.7 us (94%)
  other arithmetic  2.18 us (4%)
  between operations  0.65 us (1%)
    pallas_call x1, Pallas kernels, local(): pl.pallas_call(functools.partial(arnoldi_kernel, row_count, sub_count), o...  46.5 us
    pallas_call x1, Pallas kernels, local(): pl.pallas_call(finish_kernel, out_shape=(jax.ShapeDtypeStruct((local_rhs,...  2.17 us

profile of v3, /device:TPU:0, one launch (start us, length us, event | category | flops | bytes accessed | tf_op | source)
XLA Modules:
  0.0 51.5 jit_solution(545283406419623835)
XLA Ops:
  0.6 0.8 %pad_add_fusion.1 = s32[156]{0:T(256)S(1)} fusion(s32[12]{0:T(128)S(1)} %iota.11, s32[96]{0:T(128)} %param.19, s32[48]{0:T(128)} %param.15), kind=kLoop, calls=%fused_computation.5 | loop fusion | flops 312 | bytes 1248 | tf_op jit(solution)/shard_map/concatenate | solution.py:393
  1.4 0.7 %pad_add_fusion = s32[144]{0:T(256)S(1)} fusion(s32[96]{0:T(128)} %param.19, s32[48]{0:T(128)} %param.15), kind=kLoop, calls=%fused_computation.4 | loop fusion | flops 144 | bytes 1152 | tf_op jit(solution)/shard_map/concatenate | solution.py:392
  2.1 0.1 select_reduce_fusion
  2.2 0.6 %compare_select_fusion.chain = s32[156]{0:T(256)} fusion(s32[156]{0:T(256)S(1)} %select_reduce_fusion), kind=kLoop, calls=%fused_computation.3 | loop fusion | flops 312 | bytes 1248 | tf_op jit(solution)/shard_map/jit(_where)/select_n | solution.py:398
  2.8 46.5 %shard_map.130 = (f32[64,1536]{1,0:T(8,128)}, f32[64,1536]{1,0:T(8,128)}, f32[8,128]{1,0:T(8,128)}) custom-call(s32[48]{0:T(128)} %near_src.1, s32[96]{0:T(128)} %far_src.1, s32[96]{0:T(128)} %far_rank.1, s32[156]{0:T(256)} %compare_select_fusion.chain, s32[8,8]{1,0:T(8,128)} %send_list.1, f32[1,64]{1,0:T(1,128)} %bitcast.1, f32[64,1536]{1,0:T(8,128)} %x_ref.3, ...), custom_call_target="tpu_custom_call" | custom-call | tf_op jit(solution)/shard_map/pallas_call | solution.py:404
  49.4 2.2 %shard_map.131 = (f32[64,1536]{1,0:T(8,128)}, f32[64,1536]{1,0:T(8,128)}, f32[4,64]{1,0:T(4,128)}) custom-call(f32[64,1536]{1,0:T(8,128)} %get-tuple-element.6.second_in, f32[64,1536]{1,0:T(8,128)} %get-tuple-element.7.image_in, f32[8,128]{1,0:T(8,128)} %get-tuple-element.8.table_in, f32[64,1536]{1,0:T(8,128)} %x_ref.3), custom_call_target="tpu_custom_call" | custom-call | tf_op jit(solution)/shard_map/pallas_call | solution.py:451
  (1 shorter events, 0.0 us)

commit v4 on v3

--- a/solution.py
+++ b/solution.py
@@ -68,6 +68,17 @@
         target = lax.rem(me + offset, owners)
         return {"row": target // sub_count, "sub": lax.rem(target, sub_count)}
 
+    def each_peer(body):
+        if owners <= 16:
+            for offset in range(1, owners):
+                body(offset)
+        else:
+            def step(offset, carry):
+                body(offset)
+                return carry
+
+            lax.fori_loop(1, owners, step, 0)
+
     loads = [
         pltpu.make_async_copy(far_v_hbm, v_v, load_sem.at[0]),
         pltpu.make_async_copy(near_hbm, near_v, load_sem.at[1]),
@@ -78,13 +89,12 @@
 
     barrier = pltpu.get_barrier_semaphore()
 
-    def greet(offset, carry):
+    def greet(offset):
         pl.semaphore_signal(
             barrier, inc=1, device_id=owner_id(offset), device_id_type=pl.DeviceIdType.MESH
         )
-        return carry
-
-    lax.fori_loop(1, owners, greet, 0)
+
+    each_peer(greet)
 
     lanes = lax.broadcasted_iota(jnp.int32, (128, 128), 1)
     sublanes = lax.broadcasted_iota(jnp.int32, (128, 128), 0)
@@ -100,7 +110,7 @@
         return pl.ds(chunk * rows, rows)
 
     def send_columns(stage, chunk):
-        def one(offset, carry):
+        def one(offset):
             target = lax.rem(me + offset, owners)
             picked = send_list[me, target]
             staged[stage, chunk, offset] = rounded[stage, picked, part(chunk), :]
@@ -112,43 +122,44 @@
                 device_id=owner_id(offset),
                 device_id_type=pl.DeviceIdType.MESH,
             ).start()
-            return carry
-
-        lax.fori_loop(1, owners, one, 0)
+
+        each_peer(one)
         cols[stage][chunk][0] = rounded[stage, send_list[me, me], part(chunk), :]
 
-    def send_dots(stage, chunk, values):
+    def send_dots(stage, values):
         pad = 128 - rows * len(values)
         column = jnp.concatenate(values + ([jnp.zeros((pad, 1), jnp.float32)] if pad else []), axis=0)
         line = jnp.broadcast_to(to_line(column), (8, 128))
-        dot_send[stage, chunk] = line
-        dot_recv[stage, chunk, 0] = line
-
-        def one(offset, carry):
+        dot_send[stage] = line
+        dot_recv[stage, 0] = line
+
+        def one(offset):
             pltpu.make_async_remote_copy(
-                src_ref=dot_send.at[stage, chunk],
-                dst_ref=dot_recv.at[stage, chunk, offset],
-                send_sem=dot_send_sem.at[stage, chunk],
-                recv_sem=dot_recv_sem.at[stage, chunk],
+                src_ref=dot_send.at[stage],
+                dst_ref=dot_recv.at[stage, offset],
+                send_sem=dot_send_sem.at[stage],
+                recv_sem=dot_recv_sem.at[stage],
                 device_id=owner_id(offset),
                 device_id_type=pl.DeviceIdType.MESH,
             ).start()
-            return carry
-
-        lax.fori_loop(1, owners, one, 0)
+
+        each_peer(one)
 
     def wait_bytes(ref, sem):
         pltpu.make_async_copy(ref, ref, sem).wait()
 
-    def wait_dots(stage, chunk, count):
-        wait_bytes(
-            dot_recv.at[stage, chunk, pl.ds(1, owners - 1)], dot_recv_sem.at[stage, chunk]
-        )
+    def wait_dots(stage, count):
+        wait_bytes(dot_recv.at[stage, pl.ds(1, owners - 1)], dot_recv_sem.at[stage])
 
         def add(owner, acc):
-            return acc + dot_recv[stage, chunk, lax.rem(me + owners - owner, owners)]
-
-        line = lax.fori_loop(0, owners, add, jnp.zeros((8, 128), jnp.float32))
+            return acc + dot_recv[stage, lax.rem(me + owners - owner, owners)]
+
+        line = jnp.zeros((8, 128), jnp.float32)
+        if owners <= 16:
+            for owner in range(owners):
+                line = add(owner, line)
+        else:
+            line = lax.fori_loop(0, owners, add, line)
         column = to_column(line[0:1, :]) / panels
         return [column[k * rows : (k + 1) * rows] for k in range(count)]
 
@@ -197,7 +208,7 @@
                 )
             for j in range(UNROLL):
                 n = step * UNROLL + j
-                total[n] = results[j] + total[chain[n]]
+                total[n + 1] = results[j] + total[chain[n]]
             return carry
 
         lax.fori_loop(0, near_count // UNROLL, dense, 0)
@@ -215,7 +226,7 @@
                 )
             for j in range(UNROLL):
                 n = near_count + step * UNROLL + j
-                total[n] = results[j] + total[chain[n]]
+                total[n + 1] = results[j] + total[chain[n]]
             return carry
 
         lax.fori_loop(0, far_count // UNROLL, left_factors, 0)
@@ -248,7 +259,7 @@
     def span(q):
         return pl.ds(q * block, block)
 
-    total[blocks] = jnp.zeros((rows, block), jnp.float32)
+    total[0] = jnp.zeros((rows, block), jnp.float32)
     for q in range(local_clusters):
         rounded[0, q] = x_ref[:, span(q)].astype(jnp.bfloat16)
     shift_line = jnp.concatenate(
@@ -257,21 +268,24 @@
     shift_all = to_column(shift_line)
     shift = [shift_all[chunk * rows : (chunk + 1) * rows] for chunk in range(CHUNKS)]
     squares, inverse, coefficients = [], [], []
+    image_dots, image_means, next_dots = [], [], []
     pl.semaphore_wait(barrier, owners - 1)
 
-    def start(chunk):
-        send_columns(0, chunk)
-        acc = jnp.zeros((rows, block), jnp.float32)
-        for q in range(local_clusters):
-            value = x_ref[part(chunk), span(q)]
-            acc = acc + value * value
-        send_dots(0, chunk, [lane_sum(acc)])
+    def start_dots():
+        sums = []
+        for chunk in range(CHUNKS):
+            acc = jnp.zeros((rows, block), jnp.float32)
+            for q in range(local_clusters):
+                value = x_ref[part(chunk), span(q)]
+                acc = acc + value * value
+            sums.append(lane_sum(acc))
+        send_dots(0, sums)
 
     def first_image_of(chunk):
-        (mean_square,) = wait_dots(0, chunk, 1)
-        inv_beta = 1.0 / jnp.sqrt(mean_square + epsilon)
-        squares.append(mean_square)
-        inverse.append(inv_beta)
+        if chunk == 0:
+            squares.extend(wait_dots(0, CHUNKS))
+            inverse.extend([1.0 / jnp.sqrt(value + epsilon) for value in squares])
+        inv_beta = inverse[chunk]
         wait_bytes(part_recv.at[0, chunk], part_recv_sem.at[0, chunk])
         first_acc = jnp.zeros((rows, block), jnp.float32)
         self_acc = jnp.zeros((rows, block), jnp.float32)
@@ -284,11 +298,15 @@
             value = image[q, part(chunk), :]
             first_acc = first_acc + (x_ref[part(chunk), span(q)] * inv_beta) * value
             self_acc = self_acc + value * value
-        send_dots(1, chunk, [lane_sum(first_acc), lane_sum(self_acc)])
+        image_dots.extend([lane_sum(first_acc), lane_sum(self_acc)])
+        if chunk == CHUNKS - 1:
+            send_dots(1, image_dots)
 
     def second_image_of(chunk):
         inv_beta = inverse[chunk]
-        first_image, image_square = wait_dots(1, chunk, 2)
+        if chunk == 0:
+            image_means.extend(wait_dots(1, 2 * CHUNKS))
+        first_image, image_square = image_means[2 * chunk : 2 * chunk + 2]
         norm = squares[chunk] + epsilon
         first_square = squares[chunk] / norm
         drift = first_image - shift[chunk] * (epsilon / norm)
@@ -309,14 +327,17 @@
             image_ref[part(chunk), span(q)] = image_next
             first_acc = first_acc + first * image_next
             second_acc = second_acc + second * image_next
-        send_dots(2, chunk, [lane_sum(first_acc), lane_sum(second_acc)])
-
-    start(0)
+        next_dots.extend([lane_sum(first_acc), lane_sum(second_acc)])
+        if chunk == CHUNKS - 1:
+            send_dots(2, next_dots)
+
+    send_columns(0, 0)
+    start_dots()
     for stage, finish in ((0, first_image_of), (1, second_image_of)):
         for chunk in range(CHUNKS):
             wait_columns(stage, chunk)
             if stage == 0 and chunk + 1 < CHUNKS:
-                start(chunk + 1)
+                send_columns(0, chunk + 1)
             apply_right_and_dense(stage, chunk)
             if chunk > 0:
                 finish(chunk - 1)
@@ -324,8 +345,9 @@
         finish(CHUNKS - 1)
 
     table = [[], [], [], [], []]
+    next_means = wait_dots(2, 2 * CHUNKS)
     for chunk in range(CHUNKS):
-        cross_coef, second_coef = wait_dots(2, chunk, 2)
+        cross_coef, second_coef = next_means[2 * chunk : 2 * chunk + 2]
         values = coefficients[chunk] + (cross_coef, second_coef, cross_coef * inverse[chunk])
         for entry, value in zip(table, values):
             entry.append(value)
@@ -342,10 +364,8 @@
                 staged.at[stage, chunk, pl.ds(1, owners - 1)], col_send_sem.at[stage, chunk]
             )
             wait_bytes(part_send.at[stage, chunk], part_send_sem.at[stage, chunk])
-        for stage in range(3):
-            wait_bytes(
-                dot_recv.at[stage, chunk, pl.ds(1, owners - 1)], dot_send_sem.at[stage, chunk]
-            )
+    for stage in range(3):
+        wait_bytes(dot_recv.at[stage, pl.ds(1, owners - 1)], dot_send_sem.at[stage])
 
 
 def finish_kernel(second_in, image_in, table_in, x_ref, second_ref, resid_ref, hess_ref):
@@ -394,8 +414,7 @@
     order = jnp.arange(blocks, dtype=jnp.int32)
     place = jnp.arange(wanted.shape[0], dtype=jnp.int32)
     same = (targets[None, :] == wanted[:, None]) & (order[None, :] < place[:, None])
-    chain = jnp.max(jnp.where(same, order[None, :], -1), axis=1)
-    chain = jnp.where(chain < 0, blocks, chain)
+    chain = jnp.max(jnp.where(same, order[None, :] + 1, 0), axis=1, initial=0)
 
     smem = pl.BlockSpec(memory_space=pltpu.SMEM)
     vmem = pl.BlockSpec(memory_space=pltpu.VMEM)
@@ -423,15 +442,15 @@
             pltpu.VMEM((2, CHUNKS, sub_count - 1, clusters, rows, block), bf16),
             pltpu.VMEM((2, CHUNKS, sub_count - 1, clusters, rows, block), bf16),
             pltpu.VMEM((clusters, local_rhs, block), f32),
-            pltpu.VMEM((3, CHUNKS, 8, 128), f32),
-            pltpu.VMEM((3, CHUNKS, owners, 8, 128), f32),
+            pltpu.VMEM((3, 8, 128), f32),
+            pltpu.VMEM((3, owners, 8, 128), f32),
             pltpu.SemaphoreType.DMA((3,)),
             pltpu.SemaphoreType.DMA((2, CHUNKS)),
             pltpu.SemaphoreType.DMA((2, CHUNKS)),
             pltpu.SemaphoreType.DMA((2, CHUNKS)),
             pltpu.SemaphoreType.DMA((2, CHUNKS)),
-            pltpu.SemaphoreType.DMA((3, CHUNKS)),
-            pltpu.SemaphoreType.DMA((3, CHUNKS)),
+            pltpu.SemaphoreType.DMA((3,)),
+            pltpu.SemaphoreType.DMA((3,)),
         ],
         compiler_params=pltpu.CompilerParams(
             collective_id=0, has_side_effects=True, vmem_limit_bytes=56 * 1024 * 1024

time: 51.7 us -> 51.5 us (level)
    select_n x1 -> x0, other arithmetic: 0.57 us -> none  [local(): chain = jnp.where(chain < 0, blocks, chain)]
    max x0 -> x1, other arithmetic: none -> 0.57 us  [local(): chain = jnp.max(jnp.where(same, order[None, :] + 1, 0), axis=1, initial=0)]
where the time goes in v4:
time: 51.5 us; the launch traced here: 51.4 us
  Pallas kernels  48.5 us (94%)
  other arithmetic  2.18 us (4%)
  between operations  0.65 us (1%)
    pallas_call x1, Pallas kernels, local(): pl.pallas_call(functools.partial(arnoldi_kernel, row_count, sub_count), o...  46.4 us
    pallas_call x1, Pallas kernels, local(): pl.pallas_call(finish_kernel, out_shape=(jax.ShapeDtypeStruct((local_rhs,...  2.17 us

profile of v4, /device:TPU:0, one launch (start us, length us, event | category | flops | bytes accessed | tf_op | source)
XLA Modules:
  0.0 51.4 jit_solution(13927930392014947376)
XLA Ops:
  0.6 0.8 %pad_add_fusion.1 = s32[156]{0:T(256)S(1)} fusion(s32[12]{0:T(128)S(1)} %iota.14, s32[96]{0:T(128)} %param.19, s32[48]{0:T(128)} %param.15), kind=kLoop, calls=%fused_computation.4 | loop fusion | flops 312 | bytes 1248 | tf_op jit(solution)/shard_map/concatenate | solution.py:413
  1.4 0.7 %pad_add_fusion = (s32[144]{0:T(256)S(1)}, s32[144]{0:T(256)S(1)}) fusion(s32[96]{0:T(128)} %param.19, s32[48]{0:T(128)} %param.15), kind=kLoop, calls=%fused_computation.3 | loop fusion | flops 288 | bytes 1728 | tf_op jit(solution)/shard_map/concatenate | solution.py:412
  2.1 0.1 select_reduce_fusion
  2.3 0.6 %broadcast_maximum_fusion.chain = s32[156]{0:T(256)} fusion(s32[156]{0:T(256)S(1)} %select_reduce_fusion), kind=kLoop, calls=%fused_computation.6 | loop fusion | flops 156 | bytes 1248 | tf_op jit(solution)/shard_map/max | solution.py:417
  2.8 46.4 %shard_map.130 = (f32[64,1536]{1,0:T(8,128)}, f32[64,1536]{1,0:T(8,128)}, f32[8,128]{1,0:T(8,128)}) custom-call(s32[48]{0:T(128)} %near_src.1, s32[96]{0:T(128)} %far_src.1, s32[96]{0:T(128)} %far_rank.1, s32[156]{0:T(256)} %broadcast_maximum_fusion.chain, s32[8,8]{1,0:T(8,128)} %send_list.1, f32[1,64]{1,0:T(1,128)} %bitcast.1, f32[64,1536]{1,0:T(8,128)} %x_ref.3, ...), custom_call_target="tpu_custom_call" | custom-call | tf_op jit(solution)/shard_map/pallas_call | solution.py:423
  49.2 2.2 %shard_map.131 = (f32[64,1536]{1,0:T(8,128)}, f32[64,1536]{1,0:T(8,128)}, f32[4,64]{1,0:T(4,128)}) custom-call(f32[64,1536]{1,0:T(8,128)} %get-tuple-element.6.second_in, f32[64,1536]{1,0:T(8,128)} %get-tuple-element.7.image_in, f32[8,128]{1,0:T(8,128)} %get-tuple-element.8.table_in, f32[64,1536]{1,0:T(8,128)} %x_ref.3), custom_call_target="tpu_custom_call" | custom-call | tf_op jit(solution)/shard_map/pallas_call | solution.py:470
  (1 shorter events, 0.0 us)
